TPU v7x, 512 devices: a whole 4x4x16 slice. The times are simulated.
512 devices in a mesh: grp: 16 (over z_lo, x), fsdp: 4 (over y), tp: 8 (over z_hi, core).
Axes of the slice: x: 4, y: 4, z: 16 (z_hi: 4, z_lo: 4; z = z_hi * 4 + z_lo), core: 2. Of those that a mesh axis runs over, the one named last changes fastest.
Arguments:
- frames: bfloat16 [3072, 5120], P('fsdp', 'grp'), may hold values from -6 to 6
- projector: bfloat16 [5120, 8192], P('grp', 'tp'), may hold values from -0.078125 to 0.078125
- text_token_embedding: bfloat16 [16384, 8192], P(('grp', 'fsdp'), 'tp'), may hold values from -6 to 6
- norm_gain_vector: float32 [8192], replicated, may hold values from 0.1 to 1.9
- frozen: bfloat16 [8192, 1024], P('fsdp', 'tp'), may hold values from -0.0625 to 0.0625
- adapter_down_map: bfloat16 [8192, 64], P('fsdp'), may hold values from -0.0625 to 0.0625
- adapter_up_map: bfloat16 [64, 1024], P(None, 'tp'), may hold values from -0.75 to 0.75
- clip_frame_length: int32 [4, 16, 16], P('fsdp'), may hold values from 1 to 6, as said below
- audio_first_token: int32 [4, 16, 16], P('fsdp'), may hold values from 0 to 255, as said below
- segment_document_index: int32 [16384], P(('grp', 'fsdp')), may hold values from 0 to 255, never falling along the last dimension, each value on 1 to 256 neighbouring positions
- keep_document_flags: int32 [256], replicated, may hold values 0 or 1
- cotangent: bfloat16 [16384, 1024], P(('grp', 'fsdp'), 'tp'), may hold values from -0.046875 to 0.046875
Outputs:
- value_output: bfloat16 [16384, 1024], P(('grp', 'fsdp'), 'tp')
- projector_grad: float32 [5120, 8192], P('grp', 'tp')
- down_map_gradient: float32 [8192, 64], P('tp')
- up_map_gradient: float32 [64, 1024], P(None, 'tp')
Inputs may be any that keep to these rules, and one draw needn't show every extreme that they name: `clip_frame_length`: entry [f, g, k] is the length of clip k of frame block f * 16 + g; the 16 clips of a block sum to 48, and one of them has exactly 6 frames. `audio_first_token`: entry [f, g, k] is the first token, among the 256 tokens of block k * 4 + f, of the audio slots of clip k of frame block f * 16 + g; the 16 clips that one token block takes lie in distinct aligned windows of 16 tokens.
All inputs are finite; a program needn't handle non-finite values.
Results may differ from a plain program's by a relative error of at most 0.018.
Values may be sent and summed in bfloat16 or wider, within the bound.
No kernel may reach another device: no remote copies, remote signals or barrier semaphores. Data moves between devices by JAX's collectives and lax.ppermute only.
A program may use at most 128 MiB of HBM per device.

v0:
```python
import jax
import jax.numpy as jnp
from jax import lax
from jax.sharding import Mesh, PartitionSpec as P

adapter_scale = 2.0
norm_eps = 1e-05
GRP = ("zl", "x")
TP = ("zh", "c")
bf16, f32 = (jnp.bfloat16, jnp.float32)


def dot(a, b, ca, cb):
    return lax.dot_general(a, b, (((ca,), (cb,)), ((), ())), preferred_element_type=f32)


def exchange(blocks, axis):
    return lax.all_to_all(blocks, axis, split_axis=0, concat_axis=0, tiled=True)


def pick_entry(grid_in, position, which_axis):
    matches = lax.broadcasted_iota(jnp.int32, grid_in.shape, which_axis) == position
    return jnp.sum(jnp.where(matches, grid_in, 0), axis=which_axis)


def after(x, other):
    return x + (other[(0,) * other.ndim] * 0).astype(x.dtype)


def copies(x, n):
    return jnp.broadcast_to(x[None], (n, *x.shape))


def two_halves(v):
    hi = lax.reduce_precision(v, 8, 7)
    return (hi.astype(bf16), (v - hi).astype(bf16))


def shards(
    frames,
    projector,
    text,
    gain_all,
    frozen,
    down,
    up,
    clip_len,
    first_token,
    segment,
    keep,
    cotangent,
):
    nx, ny, nzl, ng, nt = (lax.axis_size(a) for a in ("x", "y", "zl", GRP, TP))
    grp_index, tp_index = (lax.axis_index(GRP), lax.axis_index(TP))
    x_index, y_index = (lax.axis_index("x"), lax.axis_index("y"))
    toks, width = text.shape
    cols, rank = (frozen.shape[1], down.shape[1])
    n_frames = frames.shape[0] // ng
    full_width = width * nt
    cap = 2 * n_frames // ng
    slots = ng * cap
    rows = toks + n_frames
    gain = lax.dynamic_slice_in_dim(gain_all, tp_index * width, width, 0)
    by_x = jnp.moveaxis(frames.reshape(nzl, nx, n_frames, frames.shape[1]), 1, 0)
    partial = dot(by_x.reshape(frames.shape), projector, 1, 0).astype(bf16)
    x_sum = lax.psum_scatter(partial, "x", scatter_dimension=0, tiled=True)
    all_frames = lax.all_gather(by_x.reshape(frames.shape), "y", axis=0, tiled=True)
    own_sizes = pick_entry(clip_len[0], grp_index, 0)
    before = lax.broadcasted_iota(jnp.int32, (ng, ng), 1) < lax.broadcasted_iota(
        jnp.int32, (ng, ng), 0
    )
    own_starts = jnp.sum(jnp.where(before, own_sizes[None, :], 0), axis=1)
    slot_offset = lax.broadcasted_iota(jnp.int32, (ng, cap), 1)
    frame_slot = own_starts[:, None] + slot_offset
    slot_live = slot_offset < own_sizes[:, None]
    frame_iota = lax.broadcasted_iota(jnp.int32, (ng, cap, n_frames), 2)
    sender = (
        ((frame_iota == frame_slot[:, :, None]) & slot_live[:, :, None])
        .astype(bf16)
        .reshape(slots, n_frames)
    )
    in_sizes = pick_entry(clip_len[0], grp_index, 1)
    arrive_at = pick_entry(first_token[0], grp_index, 1)
    token_iota = lax.broadcasted_iota(jnp.int32, (toks, ng, cap), 0)
    receive_mask = (token_iota == (arrive_at[:, None] + slot_offset)[None]) & (
        slot_offset < in_sizes[:, None]
    )[None]
    receiver = receive_mask.astype(bf16).reshape(toks, slots)
    is_audio = jnp.any(receive_mask, axis=(1, 2))
    doc_iota = lax.broadcasted_iota(jnp.int32, (toks, keep.shape[0]), 1)
    kept = jnp.sum(jnp.where(segment[:, None] == doc_iota, keep[None, :], 0), axis=1)
    grad_tok = cotangent * kept.astype(bf16)[:, None]
    grad_slots = exchange(dot(receiver, grad_tok, 0, 0).astype(bf16).reshape(ng, cap, cols), GRP)
    grad_frames = dot(sender, grad_slots.reshape(slots, cols), 0, 0).astype(bf16)
    grad_text = jnp.where(is_audio[:, None], jnp.zeros_like(grad_tok), grad_tok)
    grad_rows = jnp.concatenate([grad_text, grad_frames], axis=0)
    piece = width // (ny * nx)
    w_piece = lax.dynamic_index_in_dim(frozen.reshape(2, ny, nx, piece, cols), x_index, 2, False)
    down_half = lax.dynamic_slice_in_dim(down.T, lax.rem(tp_index, 2) * width, width, 1)
    down_half = jnp.moveaxis(down_half.reshape(rank, nt, cols), 1, 0).reshape(nt * rank, cols)

    def for_y(k):
        w = lax.dynamic_index_in_dim(w_piece, lax.rem(y_index + k, ny), 1, False)
        return jnp.concatenate([w.reshape(2 * piece, cols), down_half], axis=0)

    y_parts = [for_y(0)] + [
        lax.ppermute(for_y(k), "y", [(i, (i + k) % ny) for i in range(ny)]) for k in range(1, ny)
    ]
    y_parts = jnp.stack([lax.select_n(lax.rem(y_index - j + ny, ny), *y_parts) for j in range(ny)])
    wa = y_parts[:, : 2 * piece].reshape(nt, piece, cols)
    down_t = lax.dynamic_index_in_dim(y_parts[:, 2 * piece :], tp_index // 2, 0, False)
    down_t = jnp.moveaxis(down_t.reshape(nt, rank, cols), 0, 1).reshape(rank, width)
    up_rows = rank // nx
    up_piece = lax.dynamic_slice_in_dim(up, x_index * up_rows, up_rows, 0)
    text_wide = text.astype(f32)
    text_scaled = text_wide * gain[None, :]
    pair = jnp.concatenate(
        [
            (adapter_scale * dot(grad_text, up, 1, 1)).astype(bf16),
            dot(text_scaled.astype(bf16), down_t, 1, 1).astype(bf16),
        ],
        axis=1,
    )
    sq_text = dot(jnp.ones((8, width), bf16), (text_wide * text_wide).astype(bf16), 1, 1)[0]
    sent = jnp.concatenate(
        [
            wa,
            copies(jnp.concatenate([up_piece, grad_frames], axis=0), nt),
            pair.reshape(nt, toks // nt, cols),
        ],
        axis=1,
    )
    came = exchange(sent, TP)
    at = piece + up_rows
    pair = jnp.sum(came[:, at + n_frames :].astype(f32), axis=0).astype(bf16)
    blocks = exchange(x_sum.reshape(nzl, n_frames, width), "zl")
    embedded = jnp.sum(blocks.astype(f32), axis=0).astype(bf16)
    wide = embedded.astype(f32)
    scaled = wide * gain[None, :]
    grad_full = jnp.moveaxis(came[:, at : at + n_frames], 0, 1).reshape(n_frames, nt * cols)
    grad_all = lax.all_gather(grad_full, "y", axis=0, tiled=True)
    weights = jnp.moveaxis(came[:, :at], 0, 1).reshape(at, nt * cols)
    weights = lax.all_gather(weights, "x")
    up_full = weights[:, piece:].reshape(rank, nt * cols)
    weights = weights[:, :piece].reshape(nx * piece, nt * cols)
    lora_frames = (adapter_scale * dot(grad_full, up_full, 1, 1)).astype(bf16)
    spread = dot(grad_all, weights, 1, 1).astype(bf16).reshape(ny, n_frames, nx * piece)
    back = jnp.moveaxis(exchange(after(spread, embedded), "y"), 0, 1)
    grad_norm = back.reshape(n_frames, width).astype(f32)
    grad_norm = grad_norm + dot(lora_frames, down_t, 1, 0)
    weights = lax.all_gather(weights, "y", axis=0, tiled=True)
    sq_hi, sq_lo = two_halves(jnp.sum(wide * wide, axis=1, keepdims=True))
    d_hi, d_lo = two_halves(jnp.sum(scaled * grad_norm, axis=1, keepdims=True))
    low_frames = dot(scaled.astype(bf16), down_t, 1, 1).astype(bf16)
    spare = jnp.zeros((n_frames, cols - rank - 4), bf16)
    of_frames = jnp.concatenate([low_frames, sq_hi, sq_lo, d_hi, d_lo, spare], axis=1)
    n_l = toks // cols
    t_hi, t_lo = two_halves(sq_text.reshape(n_l, cols))
    spare = jnp.zeros((8 - 2 * n_l, cols), bf16)
    stats = jnp.concatenate([of_frames, t_hi, t_lo, spare, pair], axis=0)
    stats = exchange(copies(stats, nt), TP)
    pair = stats[:, n_frames + 8 :].reshape(toks, cols)
    stats = jnp.sum(stats[:, : n_frames + 8].astype(f32), axis=0)
    sq_frames = stats[:n_frames, rank : rank + 1] + stats[:n_frames, rank + 1 : rank + 2]
    dots = stats[:n_frames, rank + 2 : rank + 3] + stats[:n_frames, rank + 3 : rank + 4]
    sq_text = (
        stats[n_frames : n_frames + n_l] + stats[n_frames + n_l : n_frames + 2 * n_l]
    ).reshape(toks, 1)
    inv_rms = lax.rsqrt(jnp.concatenate([sq_text, sq_frames], axis=0) / full_width + norm_eps)
    lora = jnp.concatenate([pair[:, :rank], lora_frames], axis=0)
    low = jnp.concatenate([pair[:, rank:].astype(f32), stats[:n_frames, :rank]], axis=0)
    low_half = (low * inv_rms).astype(bf16)
    all_scaled = jnp.concatenate([text_scaled, scaled], axis=0)
    base = dot(all_scaled.astype(bf16), weights, 1, 0).astype(bf16)
    base = jnp.moveaxis(base.reshape(rows, nt, cols), 1, 0).reshape(nt * rows, cols)
    summed = lax.psum_scatter(base, TP, scatter_dimension=0, tiled=True)
    normed = (all_scaled * inv_rms).astype(bf16)
    quarter = width // ny
    down_part = dot(lora, normed, 0, 0).astype(bf16).reshape(nzl, ny * nx, width)
    up_part = (adapter_scale * dot(low_half, grad_rows, 0, 0)).astype(bf16)
    up_part = jnp.pad(up_part, ((0, 0), (0, width - cols))).reshape(nzl, ny * nx, width)
    adapters = jnp.concatenate([down_part, up_part], axis=1)
    inv_f = after(inv_rms[toks:], base)
    frame_grad = (
        inv_f * gain[None, :] * grad_norm - wide * (inv_f * inv_f * inv_f * dots / full_width)
    ).astype(bf16)
    came = exchange(jnp.concatenate([copies(frame_grad, nzl), adapters], axis=1), "zl")
    adapters = jnp.sum(came[:, n_frames:].astype(f32), axis=0).astype(bf16)
    frame_grad = came[:, :n_frames]
    n_x = nzl * n_frames
    frame_grad = jnp.moveaxis(frame_grad.reshape(n_x, ny, quarter), 1, 0)
    frame_grad = jnp.broadcast_to(frame_grad[:, None], (ny, nx, n_x, quarter))
    frame_grad = frame_grad.reshape(ny * nx, n_x, quarter)
    down_part = adapters[: ny * nx].reshape(ny * nx, ny, quarter)
    up_part = adapters[ny * nx :, :quarter].reshape(ny * nx, 1, quarter)
    spare = jnp.zeros((ny * nx, 7 - ny, quarter), bf16)
    came = exchange(jnp.concatenate([frame_grad, down_part, up_part, spare], axis=1), ("y", "x"))
    own = jnp.sum(came[:, n_x : n_x + ny + 1].astype(f32), axis=0).astype(bf16)
    own = jnp.concatenate([own[:ny].reshape(width // cols, cols), own[ny:, :cols]], axis=0)
    values = summed.astype(f32) * inv_rms + adapter_scale * dot(low_half, up, 1, 0)
    values = values.astype(bf16)
    out_slots = dot(sender, values[toks:], 1, 0).astype(bf16).reshape(nzl, 1, nx, cap, cols)
    out_slots = jnp.broadcast_to(out_slots, (nzl, ny, nx, cap, cols)).reshape(ny * ng, cap, cols)
    last = exchange(jnp.concatenate([copies(own, ny * ng), out_slots], axis=1), ("zl", "y", "x"))
    n_d = width // cols
    down_grad = last[:, :n_d].reshape(rank, width).astype(f32).T
    up_grad = last[:, n_d].astype(f32)
    all_grad = came[:, :n_x].reshape(ny * nx * n_x, quarter)
    projector_grad = after(dot(all_frames, all_grad, 0, 0), summed).astype(bf16)
    projector_grad = lax.all_gather(projector_grad, "y", axis=1, tiled=True).astype(f32)
    in_slots = last[:, -cap:].reshape(nzl, ny, nx * cap, cols)
    in_slots = lax.dynamic_index_in_dim(in_slots, y_index, 1, False).reshape(slots, cols)
    audio_values = dot(receiver, in_slots, 1, 0).astype(bf16)
    value_output = jnp.where(is_audio[:, None], audio_values, values[:toks])
    return (value_output, projector_grad, down_grad, up_grad)


def solution(mesh):
    sizes = dict(zip(mesh.axis_names, mesh.devices.shape))
    half = sizes["grp"] // 4
    mesh = Mesh(
        mesh.devices.reshape(half, 4, sizes["fsdp"], sizes["tp"] // 2, 2),
        ("zl", "x", "y", "zh", "c"),
    )
    rows = ("zl", "x", "y")
    in_specs = (
        P("y", GRP),
        P(GRP, TP),
        P(rows, TP),
        P(),
        P("y", TP),
        P("y", None),
        P(None, TP),
        P("y", None, None),
        P("y", None, None),
        P(rows),
        P(),
        P(rows, TP),
    )
    out_specs = (P(rows, TP), P(GRP, TP), P(TP, None), P(None, TP))
    return jax.shard_map(shards, mesh=mesh, in_specs=in_specs, out_specs=out_specs, check_vma=False)
```

profile of v0, /device:TPU:2, one launch (start us, length us, event | category | flops | bytes accessed | tf_op | source)
XLA Modules:
  0.0 244.0 jit_solution(16889027735061551922)
XLA Ops:
  8.1 1.1 dynamic-slice_bitcast_fusion
  9.2 0.8 constant_dynamic-slice_fusion.6
  10.1 5.1 %collective-permute-start.1 = (bf16[640,128]{1,0:T(8,128)(2,1)S(1)}, bf16[640,128]{1,0:T(8,128)(2,1)S(1)}, u32[]{:S(2)}, u32[]{:S(2)}) collective-permute-start(bf16[640,128]{1,0:T(8,128)(2,1)S(1)} %get-tuple-element.21), channel_id=1, source_target_pairs={{0,16},{8,24},{16,0},{24,8},{1,17},{9,25},{17,1},{25,9},{2,18},{10... | collective-permute-start | bytes 491528 | tf_op jit(solution)/shard_map/ppermute | solution.py:107
  15.2 3.0 %collective-permute-start.2 = (bf16[640,128]{1,0:T(8,128)(2,1)S(1)}, bf16[640,128]{1,0:T(8,128)(2,1)S(1)}, u32[]{:S(2)}, u32[]{:S(2)}) collective-permute-start(bf16[640,128]{1,0:T(8,128)(2,1)S(1)} %get-tuple-element.22), channel_id=1, source_target_pairs={{0,24},{8,0},{16,8},{24,16},{1,25},{9,1},{17,9},{25,17},{2,26},{10... | collective-permute-start | bytes 491528 | tf_op jit(solution)/shard_map/ppermute | solution.py:107
  18.2 2.9 %collective-permute-start = (bf16[640,128]{1,0:T(8,128)(2,1)S(1)}, bf16[640,128]{1,0:T(8,128)(2,1)S(1)}, u32[]{:S(2)}, u32[]{:S(2)}) collective-permute-start(bf16[640,128]{1,0:T(8,128)(2,1)S(1)} %get-tuple-element.20), channel_id=1, source_target_pairs={{0,8},{8,16},{16,24},{24,0},{1,9},{9,17},{17,25},{25,1},{2,10},{10... | collective-permute-start | bytes 491528 | tf_op jit(solution)/shard_map/ppermute | solution.py:107
  22.2 0.2 select_reduce_fusion
  22.4 0.5 fusion.73
  22.9 0.3 convolution_convert_fusion.7
  23.2 0.6 reshape.404
  23.8 8.9 %all-to-all-start.1 = ((bf16[16,6,128]{2,1,0:T(8,128)(2,1)}), bf16[16,6,128]{2,1,0:T(8,128)(2,1)S(1)}, u32[]{:S(2)}, u32[]{:S(2)}) async-start(bf16[16,6,128]{2,1,0:T(8,128)(2,1)} %reshape.404), calls=%async_computation.2 | async-start | bytes 65536 | tf_op jit(solution)/shard_map/all_to_all | solution.py:18
  32.8 0.3 copy.181
  33.2 2.1 convolution_convert_fusion
  35.8 0.1 broadcast_select_fusion
  36.1 0.7 dynamic_slice.32
  36.9 2.5 %all-to-all-done.1 = bf16[16,6,128]{2,1,0:T(8,128)(2,1)S(1)} async-done(((bf16[16,6,128]{2,1,0:T(8,128)(2,1)}), bf16[16,6,128]{2,1,0:T(8,128)(2,1)S(1)}, u32[]{:S(2)}, u32[]{:S(2)}) %all-to-all-start.1) | async-done | bytes 24608 | tf_op jit(solution)/shard_map/all_to_all | solution.py:18
  39.5 0.3 fusion.9
  39.9 0.2 select_bitcast_fusion.3
  40.2 0.2 copy-done.8
  40.4 0.5 copy-done.4
  40.9 0.3 convolution_convert_fusion.5
  41.4 35.7 %all_to_all.40 = bf16[8,160,128]{2,1,0:T(8,128)(2,1)S(1)} all-to-all(bf16[8,160,128]{2,1,0:T(8,128)(2,1)S(1)} %pad_maximum_fusion.3), channel_id=1, replica_groups=mesh['zl'=4,'x'=4,'y'=4,'zh'=4,'c'=2] {'zh','c'}, dimensions={0} | all-to-all | bytes 655360 | tf_op jit(solution)/shard_map/all_to_all | solution.py:18
  77.3 11.8 %all_gather.16 = bf16[4,80,1024]{2,1,0:T(8,128)(2,1)S(1)} all-gather(bf16[1,80,1024]{2,1,0:T(8,128)(2,1)S(1)} %all_gather_reshape.3), channel_id=1, replica_groups=mesh['zl'=4,'x'=4,'y'=4,'zh'=4,'c'=2] {'x'}, dimensions={0}, use_global_device_ids=true | all-gather | bytes 819200 | tf_op jit(solution)/shard_map/all_gather | solution.py:143
  89.2 0.8 slice.149
  90.0 5.7 %all-to-all-start = ((bf16[4,48,1024]{2,1,0:T(8,128)(2,1)}), bf16[4,48,1024]{2,1,0:T(8,128)(2,1)S(1)}, u32[]{:S(2)}, u32[]{:S(2)}) async-start(bf16[4,48,1024]{2,1,0:T(8,128)(2,1)} %bitcast.171), calls=%async_computation.1 | async-start | bytes 786432 | tf_op jit(solution)/shard_map/all_to_all | solution.py:18
  95.7 0.2 fusion.15
  96.0 13.7 %all_gather.15 = bf16[192,1024]{1,0:T(8,128)(2,1)S(1)} all-gather(bf16[48,1024]{1,0:T(8,128)(2,1)S(1)} %copy_bitcast_fusion.1), channel_id=1, replica_groups=mesh['zl'=4,'x'=4,'y'=4,'zh'=4,'c'=2] {'y'}, dimensions={0}, use_global_device_ids=true | all-gather | bytes 491520 | tf_op jit(solution)/shard_map/all_gather | solution.py:141
  109.7 0.2 fusion.10
  109.9 0.5 slice.150
  111.1 1.0 fusion.5
  112.1 3.5 %all-to-all-start.3 = ((bf16[4,48,256]{2,1,0:T(8,128)(2,1)}), bf16[4,48,256]{2,1,0:T(8,128)(2,1)S(1)}, u32[]{:S(2)}, u32[]{:S(2)}) async-start(bf16[4,48,256]{2,1,0:T(8,128)(2,1)} %bitcast.28), calls=%async_computation.4 | async-start | bytes 196608 | tf_op jit(solution)/shard_map/all_to_all | solution.py:18
  115.6 0.2 convolution_convert_fusion.8
  115.7 6.7 %all-to-all-done.3 = bf16[4,48,256]{2,1,0:T(8,128)(2,1)S(1)} async-done(((bf16[4,48,256]{2,1,0:T(8,128)(2,1)}), bf16[4,48,256]{2,1,0:T(8,128)(2,1)S(1)}, u32[]{:S(2)}, u32[]{:S(2)}) %all-to-all-start.3) | async-done | bytes 98336 | tf_op jit(solution)/shard_map/all_to_all | solution.py:18
  122.4 0.3 multiply_reduce_fusion
  123.3 0.7 broadcast_in_dim.120
  124.0 3.4 %all-to-all-start.4 = ((bf16[8,88,128]{2,1,0:T(8,128)(2,1)}), bf16[8,88,128]{2,1,0:T(8,128)(2,1)S(1)}, u32[]{:S(2)}, u32[]{:S(2)}) async-start(bf16[8,88,128]{2,1,0:T(8,128)(2,1)} %broadcast_in_dim.120), calls=%async_computation.5 | async-start | bytes 360448 | tf_op jit(solution)/shard_map/all_to_all | solution.py:18
  127.6 2.4 fusion
  130.1 0.6 slice.158
  131.4 15.7 %all-to-all-done.4 = bf16[8,88,128]{2,1,0:T(8,128)(2,1)S(1)} async-done(((bf16[8,88,128]{2,1,0:T(8,128)(2,1)}), bf16[8,88,128]{2,1,0:T(8,128)(2,1)S(1)}, u32[]{:S(2)}, u32[]{:S(2)}) %all-to-all-start.4) | async-done | bytes 180256 | tf_op jit(solution)/shard_map/all_to_all | solution.py:18
  147.0 0.2 fusion.71
  147.4 0.3 fusion.8
  147.7 0.3 convolution_convert_fusion.2
  148.5 0.9 pad_maximum_fusion.2
  149.3 3.6 %all-to-all-start.5 = ((bf16[4,80,1024]{2,1,0:T(8,128)(2,1)}), bf16[4,80,1024]{2,1,0:T(8,128)(2,1)S(1)}, u32[]{:S(2)}, u32[]{:S(2)}) async-start(bf16[4,80,1024]{2,1,0:T(8,128)(2,1)} %pad_maximum_fusion.2), calls=%async_computation.6 | async-start | bytes 1310720 | tf_op jit(solution)/shard_map/all_to_all | solution.py:18
  153.0 0.7 reduce-scatter.5.cloned.1.call-update
  153.8 0.5 all-gather.5.cloned.1.call-update
  154.4 16.3 %all-to-all-done.5 = bf16[4,80,1024]{2,1,0:T(8,128)(2,1)S(1)} async-done(((bf16[4,80,1024]{2,1,0:T(8,128)(2,1)}), bf16[4,80,1024]{2,1,0:T(8,128)(2,1)S(1)}, u32[]{:S(2)}, u32[]{:S(2)}) %all-to-all-start.5) | async-done | bytes 655392 | tf_op jit(solution)/shard_map/all_to_all | solution.py:18
  170.8 0.3 reshape.414
  171.2 0.1 broadcast_in_dim.122
  171.3 1.8 maximum_maximum_fusion
  173.2 6.0 %all-to-all-start.6 = ((bf16[16,200,256]{2,1,0:T(8,128)(2,1)}), bf16[16,200,256]{2,1,0:T(8,128)(2,1)S(1)}, u32[]{:S(2)}, u32[]{:S(2)}) async-start(bf16[16,200,256]{2,1,0:T(8,128)(2,1)} %maximum_maximum_fusion), calls=%async_computation.7 | async-start | bytes 3276800 | tf_op jit(solution)/shard_map/all_to_all | solution.py:18
  179.1 22.8 %reduce-scatter.5.cloned.1.call-done = bf16[304,128]{1,0:T(8,128)(2,1)} async-done(((bf16[2432,128]{1,0:T(8,128)(2,1)}), bf16[304,128]{1,0:T(8,128)(2,1)}) %reduce-scatter.5.cloned.1.call-update) | async-done | bytes 77840 | tf_op jit(solution)/shard_map/reduce_scatter | solution.py:176
  202.0 1.1 fusion.4
  203.1 0.2 convolution_convert_fusion.6
  203.3 0.9 all-to-all-done.6
  204.4 0.8 pad_maximum_fusion.4
  205.2 7.2 %all-to-all-start.7 = ((bf16[64,15,128]{2,1,0:T(8,128)(2,1)}), bf16[64,15,128]{2,1,0:T(8,128)(2,1)S(1)}, u32[]{:S(2)}, u32[]{:S(2)}) async-start(bf16[64,15,128]{2,1,0:T(8,128)(2,1)} %pad_maximum_fusion.4), calls=%async_computation.9 | async-start | bytes 524288 | tf_op jit(solution)/shard_map/all_to_all | solution.py:18
  212.4 1.2 slice.176
  214.2 1.3 slice.175
  215.5 3.1 %fusion.2 = bf16[320,256]{1,0:T(8,128)(2,1)S(1)} fusion(bf16[3072,256]{1,0:T(8,128)(2,1)} %bitcast.158, bf16[3072,320]{1,0:T(8,128)(2,1)} %all-gather.5.cloned.1.call-done, f32[]{:T(128)S(6)} %convert.12), kind=kOutput, calls=%fused_computation.12 | convolution fusion | flops 503480320 | bytes 3702788 | tf_op jit(solution)/shard_map/dot_general | solution.py:14
  218.7 14.4 %all_gather.19 = bf16[320,1024]{1,0:T(8,128)(2,1)S(1)} all-gather(bf16[320,256]{1,0:T(8,128)(2,1)S(1)} %fusion.2), channel_id=1, replica_groups=mesh['zl'=4,'x'=4,'y'=4,'zh'=4,'c'=2] {'y'}, dimensions={1}, use_global_device_ids=true | all-gather | bytes 819200 | tf_op jit(solution)/shard_map/all_gather | solution.py:210
  233.0 1.2 convert_element_type.229
  234.4 0.8 copy.243
  235.1 0.9 fusion.6
  236.0 0.6 slice_convert_fusion.2
  (137 shorter events, 4.7 us)
Async XLA Ops:
  8.0 25.1 %copy-start = (bf16[320,1024]{1,0:T(8,128)(2,1)S(1)}, bf16[320,1024]{1,0:T(8,128)(2,1)}, u32[]{:S(2)}) copy-start(bf16[320,1024]{1,0:T(8,128)(2,1)} %param.13) | copy-start | bytes 1966084
  8.0 13.1 %copy-start.10 = (s32[1,16,16]{2,1,0:T(8,128)S(1)}, s32[1,16,16]{2,1,0:T(8,128)}, u32[]{:S(2)}) copy-start(s32[1,16,16]{2,1,0:T(8,128)} %param.19) | copy-start | bytes 3076
  8.0 13.1 %copy-start.11 = (s32[1,16,16]{2,1,0:T(8,128)S(1)}, s32[1,16,16]{2,1,0:T(8,128)}, u32[]{:S(2)}) copy-start(s32[1,16,16]{2,1,0:T(8,128)} %param.20) | copy-start | bytes 3076
  8.0 14.1 %copy-start.12 = (s32[256]{0:T(256)S(1)}, s32[256]{0:T(256)}, u32[]{:S(2)}) copy-start(s32[256]{0:T(256)} %param.22) | copy-start | bytes 3076
  8.0 14.1 %copy-start.13 = (s32[256]{0:T(256)S(1)}, s32[256]{0:T(256)}, u32[]{:S(2)}) copy-start(s32[256]{0:T(256)} %param.21) | copy-start | bytes 3076
  8.1 14.8 %copy-start.6 = (bf16[256,128]{1,0:T(8,128)(2,1)S(1)}, bf16[256,128]{1,0:T(8,128)(2,1)}, u32[]{:S(2)}) copy-start(bf16[256,128]{1,0:T(8,128)(2,1)} %param.23) | copy-start | bytes 196612
  8.1 24.7 %copy-start.5 = (bf16[768,320]{0,1:T(8,128)(2,1)S(1)}, bf16[768,320]{0,1:T(8,128)(2,1)}, u32[]{:S(2)}) copy-start(bf16[768,320]{0,1:T(8,128)(2,1)} %param.12) | copy-start | bytes 1474564
  10.1 29.6 %collective-permute-start.1 = (bf16[640,128]{1,0:T(8,128)(2,1)S(1)}, bf16[640,128]{1,0:T(8,128)(2,1)S(1)}, u32[]{:S(2)}, u32[]{:S(2)}) collective-permute-start(bf16[640,128]{1,0:T(8,128)(2,1)S(1)} %get-tuple-element.21), channel_id=1, source_target_pairs={{0,16},{8,24},{16,0},{24,8},{1,17},{9,25},{17,1},{25,9},{2,18},{10... | collective-permute-start | bytes 491528 | tf_op jit(solution)/shard_map/ppermute | solution.py:107
  15.2 24.5 %collective-permute-start.2 = (bf16[640,128]{1,0:T(8,128)(2,1)S(1)}, bf16[640,128]{1,0:T(8,128)(2,1)S(1)}, u32[]{:S(2)}, u32[]{:S(2)}) collective-permute-start(bf16[640,128]{1,0:T(8,128)(2,1)S(1)} %get-tuple-element.22), channel_id=1, source_target_pairs={{0,24},{8,0},{16,8},{24,16},{1,25},{9,1},{17,9},{25,17},{2,26},{10... | collective-permute-start | bytes 491528 | tf_op jit(solution)/shard_map/ppermute | solution.py:107
  18.2 21.6 %collective-permute-start = (bf16[640,128]{1,0:T(8,128)(2,1)S(1)}, bf16[640,128]{1,0:T(8,128)(2,1)S(1)}, u32[]{:S(2)}, u32[]{:S(2)}) collective-permute-start(bf16[640,128]{1,0:T(8,128)(2,1)S(1)} %get-tuple-element.20), channel_id=1, source_target_pairs={{0,8},{8,16},{16,24},{24,0},{1,9},{9,17},{17,25},{25,1},{2,10},{10... | collective-permute-start | bytes 491528 | tf_op jit(solution)/shard_map/ppermute | solution.py:107
  23.8 15.7 %all-to-all-start.1 = ((bf16[16,6,128]{2,1,0:T(8,128)(2,1)}), bf16[16,6,128]{2,1,0:T(8,128)(2,1)S(1)}, u32[]{:S(2)}, u32[]{:S(2)}) async-start(bf16[16,6,128]{2,1,0:T(8,128)(2,1)} %reshape.404), calls=%async_computation.2 | async-start | bytes 65536 | tf_op jit(solution)/shard_map/all_to_all | solution.py:18
  32.7 57.3 %reduce-scatter.3.cloned.1.call-start = ((), (), s32[]{:S(2)}) async-start(), calls=%async_computation.10 | async-start | bytes 1966080 | tf_op jit(solution)/shard_map/reduce_scatter | solution.py:66
  33.1 2.2 copy-start.3
  35.3 1.5 copy-start.7
  35.3 92.3 %all-gather.3.cloned.1.call-start = ((), (), s32[]{:S(2)}) async-start(), calls=%async_computation.11 | async-start | bytes 2621440 | tf_op jit(solution)/shard_map/all_gather | solution.py:151
  39.7 0.6 copy-start.8
  39.9 1.0 copy-start.4
  90.0 21.1 %copy-start.1 = (bf16[4,64,1024]{2,1,0:T(8,128)(2,1)S(1)}, bf16[4,64,1024]{2,1,0:T(8,128)(2,1)}, u32[]{:S(2)}) copy-start(bf16[4,64,1024]{2,1,0:T(8,128)(2,1)} %slice.149) | copy-start | bytes 1572868
  90.0 19.8 %all-to-all-start = ((bf16[4,48,1024]{2,1,0:T(8,128)(2,1)}), bf16[4,48,1024]{2,1,0:T(8,128)(2,1)S(1)}, u32[]{:S(2)}, u32[]{:S(2)}) async-start(bf16[4,48,1024]{2,1,0:T(8,128)(2,1)} %bitcast.171), calls=%async_computation.1 | async-start | bytes 786432 | tf_op jit(solution)/shard_map/all_to_all | solution.py:18
  112.1 10.3 %all-to-all-start.3 = ((bf16[4,48,256]{2,1,0:T(8,128)(2,1)}), bf16[4,48,256]{2,1,0:T(8,128)(2,1)S(1)}, u32[]{:S(2)}, u32[]{:S(2)}) async-start(bf16[4,48,256]{2,1,0:T(8,128)(2,1)} %bitcast.28), calls=%async_computation.4 | async-start | bytes 196608 | tf_op jit(solution)/shard_map/all_to_all | solution.py:18
  124.0 23.0 %all-to-all-start.4 = ((bf16[8,88,128]{2,1,0:T(8,128)(2,1)}), bf16[8,88,128]{2,1,0:T(8,128)(2,1)S(1)}, u32[]{:S(2)}, u32[]{:S(2)}) async-start(bf16[8,88,128]{2,1,0:T(8,128)(2,1)} %broadcast_in_dim.120), calls=%async_computation.5 | async-start | bytes 360448 | tf_op jit(solution)/shard_map/all_to_all | solution.py:18
  130.0 17.4 %copy-start.9 = (bf16[48,128]{1,0:T(8,128)(2,1)S(1)}, bf16[48,128]{1,0:T(8,128)(2,1)}, u32[]{:S(2)}) copy-start(bf16[48,128]{1,0:T(8,128)(2,1)} %copy-done.8) | copy-start | bytes 36868
  130.1 18.3 %copy-start.2 = (bf16[38,8,8,128]{3,2,0,1:T(8,128)(2,1)}, bf16[38,8,8,128]{3,2,0,1:T(8,128)(2,1)S(1)}, u32[]{:S(2)}) copy-start(bf16[38,8,8,128]{3,2,0,1:T(8,128)(2,1)S(1)} %copy.242) | copy-start | bytes 1867780
  149.3 21.3 %all-to-all-start.5 = ((bf16[4,80,1024]{2,1,0:T(8,128)(2,1)}), bf16[4,80,1024]{2,1,0:T(8,128)(2,1)S(1)}, u32[]{:S(2)}, u32[]{:S(2)}) async-start(bf16[4,80,1024]{2,1,0:T(8,128)(2,1)} %pad_maximum_fusion.2), calls=%async_computation.6 | async-start | bytes 1310720 | tf_op jit(solution)/shard_map/all_to_all | solution.py:18
  153.0 49.0 %reduce-scatter.5.cloned.1.call-start = ((), (), s32[]{:S(2)}) async-start(), calls=%async_computation.12 | async-start | bytes 700416 | tf_op jit(solution)/shard_map/reduce_scatter | solution.py:176
  153.7 61.8 %all-gather.5.cloned.1.call-start = ((), (), s32[]{:S(2)}) async-start(), calls=%async_computation.13 | async-start | bytes 2949120 | tf_op jit(solution)/shard_map/all_gather | solution.py:67
  173.2 29.9 %copy-start.14 = (pred[96]{0:T(512)(128)(4,1)S(1)}, pred[96]{0:T(512)(128)(4,1)}, u32[]{:S(2)}) copy-start(pred[96]{0:T(512)(128)(4,1)} %get-tuple-element.37) | copy-start | bytes 292
  173.2 31.1 %all-to-all-start.6 = ((bf16[16,200,256]{2,1,0:T(8,128)(2,1)}), bf16[16,200,256]{2,1,0:T(8,128)(2,1)S(1)}, u32[]{:S(2)}, u32[]{:S(2)}) async-start(bf16[16,200,256]{2,1,0:T(8,128)(2,1)} %maximum_maximum_fusion), calls=%async_computation.7 | async-start | bytes 3276800 | tf_op jit(solution)/shard_map/all_to_all | solution.py:18
  205.2 29.1 %all-to-all-start.7 = ((bf16[64,15,128]{2,1,0:T(8,128)(2,1)}), bf16[64,15,128]{2,1,0:T(8,128)(2,1)S(1)}, u32[]{:S(2)}, u32[]{:S(2)}) async-start(bf16[64,15,128]{2,1,0:T(8,128)(2,1)} %pad_maximum_fusion.4), calls=%async_computation.9 | async-start | bytes 524288 | tf_op jit(solution)/shard_map/all_to_all | solution.py:18
Sparse Core Ops, SparseCore 0:
  36.4 33.1 reduce-scatter.2
  156.6 45.2 reduce-scatter.4
Sparse Core Ops, SparseCore 1:
  90.1 34.2 all-gather.2
  156.3 50.3 all-gather.4
where the time goes:
time: 245 us; the launch traced here: 244 us
  blocking collectives  75.6 us (31%)
  waiting for transfers between devices  66.2 us (27%)
  starting transfers between devices  49.3 us (20%)
  between operations  18.4 us (8%)
  local copies, waits for them, and re-layouts  13.3 us (5%)
  matrix products  13.2 us (5%)
  other arithmetic  8.08 us (3%)
    all_to_all x7, waiting for transfers between devices, exchange(): return lax.all_to_all(blocks, axis, split_axis=0, concat_axis=0, tiled=True)  42 us
    all_to_all x7, starting transfers between devices, exchange(): return lax.all_to_all(blocks, axis, split_axis=0, concat_axis=0, tiled=True)  38.2 us
    all_to_all x1, blocking collectives, exchange(): return lax.all_to_all(blocks, axis, split_axis=0, concat_axis=0, tiled=True)  35.7 us
    reduce_scatter x1, waiting for transfers between devices, shards(): summed = lax.psum_scatter(base, TP, scatter_dimension=0, tiled=True)  22.8 us
    all_gather x1, blocking collectives, shards(): lax.all_gather(projector_grad, 'y', axis=1, tiled=True).astype(f32)  14.4 us
    all_gather x1, blocking collectives, shards(): grad_all = lax.all_gather(grad_full, 'y', axis=0, tiled=True)  13.7 us
    dot_general x17, matrix products, dot(): lax.dot_general(a, b, (((ca,), (cb,)), ((), ())), preferred_element_type=...  13.2 us
    all_gather x1, blocking collectives, shards(): weights = lax.all_gather(weights, 'x')  11.8 us
  transfers between devices with their start and end apart: 14, of which 6 were waited for; matrix products, arithmetic and copies ran while one was open for 11% of the time, Pallas kernels for 0%

commit v1 on v0

--- a/solution.py
+++ b/solution.py
@@ -207,7 +207,9 @@
     up_grad = last[:, n_d].astype(f32)
     all_grad = came[:, :n_x].reshape(ny * nx * n_x, quarter)
     projector_grad = after(dot(all_frames, all_grad, 0, 0), summed).astype(bf16)
-    projector_grad = lax.all_gather(projector_grad, "y", axis=1, tiled=True).astype(f32)
+    projector_grad = jnp.concatenate(
+        lax.all_to_all(jnp.stack([projector_grad] * lax.axis_size("y")), "y", 0, 0), axis=1
+    ).astype(f32)
     in_slots = last[:, -cap:].reshape(nzl, ny, nx * cap, cols)
     in_slots = lax.dynamic_index_in_dim(in_slots, y_index, 1, False).reshape(slots, cols)
     audio_values = dot(receiver, in_slots, 1, 0).astype(bf16)

time: 245 us -> 257 us (1.049)
  waiting for transfers between devices: 66.2 us -> 84.2 us
  blocking collectives: 75.6 us -> 62.3 us
  starting transfers between devices: 49.3 us -> 53.9 us
  local copies, waits for them, and re-layouts: 13.3 us -> 17 us
    all_to_all x7, waiting for transfers between devices: 42 us -> 75 us  [exchange(): return lax.all_to_all(blocks, axis, split_axis=0, concat_axis=0, tiled=True)]
    reduce_scatter x1, waiting for transfers between devices: 22.8 us -> 0.01 us  [shards(): summed = lax.psum_scatter(base, TP, scatter_dimension=0, tiled=True)]
    all_gather x1 -> x0, blocking collectives: 14.4 us -> none  [shards(): lax.all_gather(projector_grad, 'y', axis=1, tiled=True).astype(f32)]
    all_to_all x0 -> x1, waiting for transfers between devices: none -> 8.52 us  [shards(): lax.all_to_all(jnp.stack([projector_grad] * lax.axis_size('y')), 'y', 0, 0)]
    all_to_all x0 -> x1, starting transfers between devices: none -> 3.48 us  [shards(): lax.all_to_all(jnp.stack([projector_grad] * lax.axis_size('y')), 'y', 0, 0)]
  transfers between devices with their start and end apart: 14 -> 15, of which waited for: 6 -> 7; matrix products, arithmetic and copies ran while one was open for 11% -> 11% of each run, Pallas kernels for 0% -> 0%
where the time goes in v1:
time: 257 us; the launch traced here: 256 us
  waiting for transfers between devices  84.2 us (33%)
  blocking collectives  62.3 us (24%)
  starting transfers between devices  53.9 us (21%)
  between operations  18.3 us (7%)
  local copies, waits for them, and re-layouts  17 us (7%)
  matrix products  13.2 us (5%)
  other arithmetic  7.13 us (3%)
    all_to_all x7, waiting for transfers between devices, exchange(): return lax.all_to_all(blocks, axis, split_axis=0, concat_axis=0, tiled=True)  75 us
    all_to_all x7, starting transfers between devices, exchange(): return lax.all_to_all(blocks, axis, split_axis=0, concat_axis=0, tiled=True)  39.4 us
    all_to_all x1, blocking collectives, exchange(): return lax.all_to_all(blocks, axis, split_axis=0, concat_axis=0, tiled=True)  35.7 us
    all_gather x1, blocking collectives, shards(): grad_all = lax.all_gather(grad_full, 'y', axis=0, tiled=True)  13.7 us
    dot_general x17, matrix products, dot(): lax.dot_general(a, b, (((ca,), (cb,)), ((), ())), preferred_element_type=...  13.2 us
    all_gather x1, blocking collectives, shards(): weights = lax.all_gather(weights, 'x')  12.9 us
    ppermute x3, starting transfers between devices, shards(): lax.ppermute(for_y(k), 'y', [(i, (i + k) % ny) for i in range(ny)])  10.9 us
    all_to_all x1, waiting for transfers between devices, shards(): lax.all_to_all(jnp.stack([projector_grad] * lax.axis_size('y')), 'y', 0, 0)  8.52 us
  transfers between devices with their start and end apart: 15, of which 7 were waited for; matrix products, arithmetic and copies ran while one was open for 11% of the time, Pallas kernels for 0%

profile of v1, /device:TPU:2, one launch (start us, length us, event | category | flops | bytes accessed | tf_op | source)
XLA Modules:
  0.0 256.1 jit_solution(13364328456596634284)
XLA Ops:
  8.1 1.1 dynamic-slice_bitcast_fusion
  9.2 0.8 constant_dynamic-slice_fusion.6
  10.1 0.7 pad_maximum_fusion.6
  10.8 5.1 %collective-permute-start.1 = (bf16[640,128]{1,0:T(8,128)(2,1)}, bf16[640,128]{1,0:T(8,128)(2,1)S(1)}, u32[]{:S(2)}, u32[]{:S(2)}) collective-permute-start(bf16[640,128]{1,0:T(8,128)(2,1)} %get-tuple-element.21), channel_id=1, source_target_pairs={{0,16},{8,24},{16,0},{24,8},{1,17},{9,25},{17,1},{25,9},{2,18},{10... | collective-permute-start | bytes 491528 | tf_op jit(solution)/shard_map/ppermute | solution.py:107
  15.9 3.0 %collective-permute-start.2 = (bf16[640,128]{1,0:T(8,128)(2,1)S(1)}, bf16[640,128]{1,0:T(8,128)(2,1)S(1)}, u32[]{:S(2)}, u32[]{:S(2)}) collective-permute-start(bf16[640,128]{1,0:T(8,128)(2,1)S(1)} %get-tuple-element.22), channel_id=1, source_target_pairs={{0,24},{8,0},{16,8},{24,16},{1,25},{9,1},{17,9},{25,17},{2,26},{10... | collective-permute-start | bytes 491528 | tf_op jit(solution)/shard_map/ppermute | solution.py:107
  18.9 2.9 %collective-permute-start = (bf16[640,128]{1,0:T(8,128)(2,1)S(1)}, bf16[640,128]{1,0:T(8,128)(2,1)S(1)}, u32[]{:S(2)}, u32[]{:S(2)}) collective-permute-start(bf16[640,128]{1,0:T(8,128)(2,1)S(1)} %get-tuple-element.20), channel_id=1, source_target_pairs={{0,8},{8,16},{16,24},{24,0},{1,9},{9,17},{17,25},{25,1},{2,10},{10... | collective-permute-start | bytes 491528 | tf_op jit(solution)/shard_map/ppermute | solution.py:107
  22.8 0.2 select_reduce_fusion
  23.1 0.3 convolution_convert_fusion.7
  23.3 0.6 reshape.410
  24.0 8.9 %all-to-all-start.1 = ((bf16[16,6,128]{2,1,0:T(8,128)(2,1)}), bf16[16,6,128]{2,1,0:T(8,128)(2,1)S(1)}, u32[]{:S(2)}, u32[]{:S(2)}) async-start(bf16[16,6,128]{2,1,0:T(8,128)(2,1)} %reshape.410), calls=%async_computation.2 | async-start | bytes 65536 | tf_op jit(solution)/shard_map/all_to_all | solution.py:18
  32.9 0.3 copy.210
  33.3 2.1 convolution_convert_fusion
  36.3 0.7 dynamic_slice.32
  37.1 2.5 all-to-all-done.1
  39.6 0.3 fusion.9
  40.0 0.2 select_bitcast_fusion.3
  40.4 0.9 copy-done.3
  41.3 0.3 convolution_convert_fusion.5
  41.8 35.7 %all_to_all.45 = bf16[8,160,128]{2,1,0:T(8,128)(2,1)S(1)} all-to-all(bf16[8,160,128]{2,1,0:T(8,128)(2,1)S(1)} %pad_maximum_fusion.3), channel_id=1, replica_groups=mesh['zl'=4,'x'=4,'y'=4,'zh'=4,'c'=2] {'zh','c'}, dimensions={0} | all-to-all | bytes 655360 | tf_op jit(solution)/shard_map/all_to_all | solution.py:18
  77.6 12.9 %all_gather.13 = bf16[4,80,1024]{2,1,0:T(8,128)(2,1)S(1)} all-gather(bf16[1,80,1024]{2,1,0:T(8,128)(2,1)S(1)} %all_gather_reshape.3), channel_id=1, replica_groups=mesh['zl'=4,'x'=4,'y'=4,'zh'=4,'c'=2] {'x'}, dimensions={0}, use_global_device_ids=true | all-gather | bytes 819200 | tf_op jit(solution)/shard_map/all_gather | solution.py:143
  90.6 0.8 slice.149
  91.5 4.6 %all-to-all-start = ((bf16[4,48,1024]{2,1,0:T(8,128)(2,1)}), bf16[4,48,1024]{2,1,0:T(8,128)(2,1)S(1)}, u32[]{:S(2)}, u32[]{:S(2)}) async-start(bf16[4,48,1024]{2,1,0:T(8,128)(2,1)} %bitcast.176), calls=%async_computation.1 | async-start | bytes 786432 | tf_op jit(solution)/shard_map/all_to_all | solution.py:18
  96.0 0.2 fusion.15
  96.3 13.7 %all_gather.12 = bf16[192,1024]{1,0:T(8,128)(2,1)S(1)} all-gather(bf16[48,1024]{1,0:T(8,128)(2,1)S(1)} %copy_bitcast_fusion.1), channel_id=1, replica_groups=mesh['zl'=4,'x'=4,'y'=4,'zh'=4,'c'=2] {'y'}, dimensions={0}, use_global_device_ids=true | all-gather | bytes 491520 | tf_op jit(solution)/shard_map/all_gather | solution.py:141
  110.0 0.2 fusion.10
  110.3 0.5 slice.150
  111.5 1.0 fusion.5
  112.4 3.4 %all-to-all-start.3 = ((bf16[4,48,256]{2,1,0:T(8,128)(2,1)}), bf16[4,48,256]{2,1,0:T(8,128)(2,1)S(1)}, u32[]{:S(2)}, u32[]{:S(2)}) async-start(bf16[4,48,256]{2,1,0:T(8,128)(2,1)} %bitcast.28), calls=%async_computation.4 | async-start | bytes 196608 | tf_op jit(solution)/shard_map/all_to_all | solution.py:18
  115.9 0.2 convolution_convert_fusion.8
  116.0 6.7 %all-to-all-done.3 = bf16[4,48,256]{2,1,0:T(8,128)(2,1)S(1)} async-done(((bf16[4,48,256]{2,1,0:T(8,128)(2,1)}), bf16[4,48,256]{2,1,0:T(8,128)(2,1)S(1)}, u32[]{:S(2)}, u32[]{:S(2)}) %all-to-all-start.3) | async-done | bytes 98336 | tf_op jit(solution)/shard_map/all_to_all | solution.py:18
  122.7 0.3 multiply_reduce_fusion
  123.6 0.7 broadcast_in_dim.120
  124.3 3.4 %all-to-all-start.4 = ((bf16[8,88,128]{2,1,0:T(8,128)(2,1)}), bf16[8,88,128]{2,1,0:T(8,128)(2,1)S(1)}, u32[]{:S(2)}, u32[]{:S(2)}) async-start(bf16[8,88,128]{2,1,0:T(8,128)(2,1)} %broadcast_in_dim.120), calls=%async_computation.5 | async-start | bytes 360448 | tf_op jit(solution)/shard_map/all_to_all | solution.py:18
  127.9 2.4 fusion
  130.3 0.9 copy.273
  131.3 1.2 slice.158
  133.2 14.2 %all-to-all-done.4 = bf16[8,88,128]{2,1,0:T(8,128)(2,1)S(1)} async-done(((bf16[8,88,128]{2,1,0:T(8,128)(2,1)}), bf16[8,88,128]{2,1,0:T(8,128)(2,1)S(1)}, u32[]{:S(2)}, u32[]{:S(2)}) %all-to-all-start.4) | async-done | bytes 180256 | tf_op jit(solution)/shard_map/all_to_all | solution.py:18
  147.3 0.2 fusion.71
  147.7 0.3 fusion.8
  148.0 0.3 convolution_convert_fusion.2
  148.7 0.9 pad_maximum_fusion.2
  149.6 3.6 %all-to-all-start.5 = ((bf16[4,80,1024]{2,1,0:T(8,128)(2,1)}), bf16[4,80,1024]{2,1,0:T(8,128)(2,1)S(1)}, u32[]{:S(2)}, u32[]{:S(2)}) async-start(bf16[4,80,1024]{2,1,0:T(8,128)(2,1)} %pad_maximum_fusion.2), calls=%async_computation.6 | async-start | bytes 1310720 | tf_op jit(solution)/shard_map/all_to_all | solution.py:18
  153.3 0.6 all-gather.5.cloned.1.call-update
  153.9 23.1 %all-to-all-done.5 = bf16[4,80,1024]{2,1,0:T(8,128)(2,1)S(1)} async-done(((bf16[4,80,1024]{2,1,0:T(8,128)(2,1)}), bf16[4,80,1024]{2,1,0:T(8,128)(2,1)S(1)}, u32[]{:S(2)}, u32[]{:S(2)}) %all-to-all-start.5) | async-done | bytes 655392 | tf_op jit(solution)/shard_map/all_to_all | solution.py:18
  177.1 0.3 reshape.420
  177.5 0.1 broadcast_in_dim.122
  177.6 1.8 maximum_maximum_fusion
  179.5 5.1 %all-to-all-start.6 = ((bf16[16,200,256]{2,1,0:T(8,128)(2,1)}), bf16[16,200,256]{2,1,0:T(8,128)(2,1)S(1)}, u32[]{:S(2)}, u32[]{:S(2)}) async-start(bf16[16,200,256]{2,1,0:T(8,128)(2,1)} %maximum_maximum_fusion), calls=%async_computation.7 | async-start | bytes 3276800 | tf_op jit(solution)/shard_map/all_to_all | solution.py:18
  184.6 1.2 slice.176
  186.4 1.1 fusion.4
  187.6 18.9 %all-to-all-done.6 = bf16[16,200,256]{2,1,0:T(8,128)(2,1)S(1)} async-done(((bf16[16,200,256]{2,1,0:T(8,128)(2,1)}), bf16[16,200,256]{2,1,0:T(8,128)(2,1)S(1)}, u32[]{:S(2)}, u32[]{:S(2)}) %all-to-all-start.6) | async-done | bytes 1638432 | tf_op jit(solution)/shard_map/all_to_all | solution.py:18
  206.4 1.3 slice.175
  207.7 3.1 %fusion.2 = bf16[320,256]{1,0:T(8,128)(2,1)S(1)} fusion(bf16[3072,256]{1,0:T(8,128)(2,1)} %bitcast.162, bf16[3072,320]{1,0:T(8,128)(2,1)} %all-gather.5.cloned.1.call-done, f32[]{:T(128)S(6)} %convert.14), kind=kOutput, calls=%fused_computation.13 | convolution fusion | flops 503480320 | bytes 3702788 | tf_op jit(solution)/shard_map/dot_general | solution.py:14
  210.9 0.9 stack.27
  211.8 3.5 %all-to-all-start.8 = ((bf16[4,320,256]{2,1,0:T(8,128)(2,1)}), bf16[4,320,256]{2,1,0:T(8,128)(2,1)S(1)}, u32[]{:S(2)}, u32[]{:S(2)}) async-start(bf16[4,320,256]{2,1,0:T(8,128)(2,1)} %stack.27), calls=%async_computation.10 | async-start | bytes 1310720 | tf_op jit(solution)/shard_map/all_to_all | solution.py:211
  215.3 0.2 convolution_convert_fusion.6
  215.7 0.8 pad_maximum_fusion.4
  216.4 8.5 %all-to-all-done.8 = bf16[4,320,256]{2,1,0:T(8,128)(2,1)S(1)} async-done(((bf16[4,320,256]{2,1,0:T(8,128)(2,1)}), bf16[4,320,256]{2,1,0:T(8,128)(2,1)S(1)}, u32[]{:S(2)}, u32[]{:S(2)}) %all-to-all-start.8) | async-done | bytes 655392 | tf_op jit(solution)/shard_map/all_to_all | solution.py:211
  225.0 10.4 %all-to-all-start.7 = ((bf16[64,15,128]{2,1,0:T(8,128)(2,1)}), bf16[64,15,128]{2,1,0:T(8,128)(2,1)S(1)}, u32[]{:S(2)}, u32[]{:S(2)}) async-start(bf16[64,15,128]{2,1,0:T(8,128)(2,1)} %pad_maximum_fusion.4), calls=%async_computation.9 | async-start | bytes 524288 | tf_op jit(solution)/shard_map/all_to_all | solution.py:18
  235.5 1.2 copy.250
  236.7 9.6 %all-to-all-done.7 = bf16[64,15,128]{2,1,0:T(8,128)(2,1)S(1)} async-done(((bf16[64,15,128]{2,1,0:T(8,128)(2,1)}), bf16[64,15,128]{2,1,0:T(8,128)(2,1)S(1)}, u32[]{:S(2)}, u32[]{:S(2)}) %all-to-all-start.7) | async-done | bytes 245792 | tf_op jit(solution)/shard_map/all_to_all | solution.py:18
  246.5 0.8 copy.274
  247.2 0.9 fusion.6
  248.1 0.6 slice_convert_fusion.2
  (132 shorter events, 4.8 us)
Async XLA Ops:
  8.0 25.3 %copy-start = (bf16[320,1024]{1,0:T(8,128)(2,1)S(1)}, bf16[320,1024]{1,0:T(8,128)(2,1)}, u32[]{:S(2)}) copy-start(bf16[320,1024]{1,0:T(8,128)(2,1)} %param.13) | copy-start | bytes 1966084
  8.0 13.8 %copy-start.7 = (s32[1,16,16]{2,1,0:T(8,128)S(1)}, s32[1,16,16]{2,1,0:T(8,128)}, u32[]{:S(2)}) copy-start(s32[1,16,16]{2,1,0:T(8,128)} %param.19) | copy-start | bytes 3076
  8.0 13.8 %copy-start.8 = (s32[1,16,16]{2,1,0:T(8,128)S(1)}, s32[1,16,16]{2,1,0:T(8,128)}, u32[]{:S(2)}) copy-start(s32[1,16,16]{2,1,0:T(8,128)} %param.20) | copy-start | bytes 3076
  8.0 14.8 %copy-start.9 = (s32[256]{0:T(256)S(1)}, s32[256]{0:T(256)}, u32[]{:S(2)}) copy-start(s32[256]{0:T(256)} %param.22) | copy-start | bytes 3076
  8.0 14.8 %copy-start.10 = (s32[256]{0:T(256)S(1)}, s32[256]{0:T(256)}, u32[]{:S(2)}) copy-start(s32[256]{0:T(256)} %param.21) | copy-start | bytes 3076
  8.1 15.0 %copy-start.5 = (bf16[256,128]{1,0:T(8,128)(2,1)S(1)}, bf16[256,128]{1,0:T(8,128)(2,1)}, u32[]{:S(2)}) copy-start(bf16[256,128]{1,0:T(8,128)(2,1)} %param.23) | copy-start | bytes 196612
  8.1 24.8 %copy-start.4 = (bf16[768,320]{0,1:T(8,128)(2,1)S(1)}, bf16[768,320]{0,1:T(8,128)(2,1)}, u32[]{:S(2)}) copy-start(bf16[768,320]{0,1:T(8,128)(2,1)} %param.12) | copy-start | bytes 1474564
  10.8 29.1 %collective-permute-start.1 = (bf16[640,128]{1,0:T(8,128)(2,1)}, bf16[640,128]{1,0:T(8,128)(2,1)S(1)}, u32[]{:S(2)}, u32[]{:S(2)}) collective-permute-start(bf16[640,128]{1,0:T(8,128)(2,1)} %get-tuple-element.21), channel_id=1, source_target_pairs={{0,16},{8,24},{16,0},{24,8},{1,17},{9,25},{17,1},{25,9},{2,18},{10... | collective-permute-start | bytes 491528 | tf_op jit(solution)/shard_map/ppermute | solution.py:107
  15.9 24.0 %collective-permute-start.2 = (bf16[640,128]{1,0:T(8,128)(2,1)S(1)}, bf16[640,128]{1,0:T(8,128)(2,1)S(1)}, u32[]{:S(2)}, u32[]{:S(2)}) collective-permute-start(bf16[640,128]{1,0:T(8,128)(2,1)S(1)} %get-tuple-element.22), channel_id=1, source_target_pairs={{0,24},{8,0},{16,8},{24,16},{1,25},{9,1},{17,9},{25,17},{2,26},{10... | collective-permute-start | bytes 491528 | tf_op jit(solution)/shard_map/ppermute | solution.py:107
  18.9 21.1 %collective-permute-start = (bf16[640,128]{1,0:T(8,128)(2,1)S(1)}, bf16[640,128]{1,0:T(8,128)(2,1)S(1)}, u32[]{:S(2)}, u32[]{:S(2)}) collective-permute-start(bf16[640,128]{1,0:T(8,128)(2,1)S(1)} %get-tuple-element.20), channel_id=1, source_target_pairs={{0,8},{8,16},{16,24},{24,0},{1,9},{9,17},{17,25},{25,1},{2,10},{10... | collective-permute-start | bytes 491528 | tf_op jit(solution)/shard_map/ppermute | solution.py:107
  24.0 15.7 %all-to-all-start.1 = ((bf16[16,6,128]{2,1,0:T(8,128)(2,1)}), bf16[16,6,128]{2,1,0:T(8,128)(2,1)S(1)}, u32[]{:S(2)}, u32[]{:S(2)}) async-start(bf16[16,6,128]{2,1,0:T(8,128)(2,1)} %reshape.410), calls=%async_computation.2 | async-start | bytes 65536 | tf_op jit(solution)/shard_map/all_to_all | solution.py:18
  32.9 58.6 %reduce-scatter.3.cloned.1.call-start = ((), (), s32[]{:S(2)}) async-start(), calls=%async_computation.11 | async-start | bytes 1966080 | tf_op jit(solution)/shard_map/reduce_scatter | solution.py:66
  33.3 2.2 copy-start.2
  35.4 1.5 copy-start.6
  35.5 92.5 %all-gather.3.cloned.1.call-start = ((), (), s32[]{:S(2)}) async-start(), calls=%async_computation.12 | async-start | bytes 2621440 | tf_op jit(solution)/shard_map/all_gather | solution.py:151
  40.2 1.0 copy-start.3
  91.4 20.0 %copy-start.1 = (bf16[4,64,1024]{2,1,0:T(8,128)(2,1)S(1)}, bf16[4,64,1024]{2,1,0:T(8,128)(2,1)}, u32[]{:S(2)}) copy-start(bf16[4,64,1024]{2,1,0:T(8,128)(2,1)} %slice.149) | copy-start | bytes 1572868
  91.5 18.7 %all-to-all-start = ((bf16[4,48,1024]{2,1,0:T(8,128)(2,1)}), bf16[4,48,1024]{2,1,0:T(8,128)(2,1)S(1)}, u32[]{:S(2)}, u32[]{:S(2)}) async-start(bf16[4,48,1024]{2,1,0:T(8,128)(2,1)} %bitcast.176), calls=%async_computation.1 | async-start | bytes 786432 | tf_op jit(solution)/shard_map/all_to_all | solution.py:18
  112.4 10.3 %all-to-all-start.3 = ((bf16[4,48,256]{2,1,0:T(8,128)(2,1)}), bf16[4,48,256]{2,1,0:T(8,128)(2,1)S(1)}, u32[]{:S(2)}, u32[]{:S(2)}) async-start(bf16[4,48,256]{2,1,0:T(8,128)(2,1)} %bitcast.28), calls=%async_computation.4 | async-start | bytes 196608 | tf_op jit(solution)/shard_map/all_to_all | solution.py:18
  124.3 23.0 %all-to-all-start.4 = ((bf16[8,88,128]{2,1,0:T(8,128)(2,1)}), bf16[8,88,128]{2,1,0:T(8,128)(2,1)S(1)}, u32[]{:S(2)}, u32[]{:S(2)}) async-start(bf16[8,88,128]{2,1,0:T(8,128)(2,1)} %broadcast_in_dim.120), calls=%async_computation.5 | async-start | bytes 360448 | tf_op jit(solution)/shard_map/all_to_all | solution.py:18
  127.7 56.9 %reduce-scatter.5.cloned.1.call-start = ((), (), s32[]{:S(2)}) async-start(), calls=%async_computation.13 | async-start | bytes 700416 | tf_op jit(solution)/shard_map/reduce_scatter | solution.py:176
  149.6 27.4 %all-to-all-start.5 = ((bf16[4,80,1024]{2,1,0:T(8,128)(2,1)}), bf16[4,80,1024]{2,1,0:T(8,128)(2,1)S(1)}, u32[]{:S(2)}, u32[]{:S(2)}) async-start(bf16[4,80,1024]{2,1,0:T(8,128)(2,1)} %pad_maximum_fusion.2), calls=%async_computation.6 | async-start | bytes 1310720 | tf_op jit(solution)/shard_map/all_to_all | solution.py:18
  153.3 54.5 %all-gather.5.cloned.1.call-start = ((), (), s32[]{:S(2)}) async-start(), calls=%async_computation.14 | async-start | bytes 2949120 | tf_op jit(solution)/shard_map/all_gather | solution.py:67
  179.5 27.0 %all-to-all-start.6 = ((bf16[16,200,256]{2,1,0:T(8,128)(2,1)}), bf16[16,200,256]{2,1,0:T(8,128)(2,1)S(1)}, u32[]{:S(2)}, u32[]{:S(2)}) async-start(bf16[16,200,256]{2,1,0:T(8,128)(2,1)} %maximum_maximum_fusion), calls=%async_computation.7 | async-start | bytes 3276800 | tf_op jit(solution)/shard_map/all_to_all | solution.py:18
  211.8 13.2 %all-to-all-start.8 = ((bf16[4,320,256]{2,1,0:T(8,128)(2,1)}), bf16[4,320,256]{2,1,0:T(8,128)(2,1)S(1)}, u32[]{:S(2)}, u32[]{:S(2)}) async-start(bf16[4,320,256]{2,1,0:T(8,128)(2,1)} %stack.27), calls=%async_computation.10 | async-start | bytes 1310720 | tf_op jit(solution)/shard_map/all_to_all | solution.py:211
  225.0 21.4 %all-to-all-start.7 = ((bf16[64,15,128]{2,1,0:T(8,128)(2,1)}), bf16[64,15,128]{2,1,0:T(8,128)(2,1)S(1)}, u32[]{:S(2)}, u32[]{:S(2)}) async-start(bf16[64,15,128]{2,1,0:T(8,128)(2,1)} %pad_maximum_fusion.4), calls=%async_computation.9 | async-start | bytes 524288 | tf_op jit(solution)/shard_map/all_to_all | solution.py:18
Sparse Core Ops, SparseCore 0:
  36.5 33.2 reduce-scatter.2
  131.4 52.1 reduce-scatter.4
Sparse Core Ops, SparseCore 1:
  91.5 33.1 all-gather.2
  155.8 37.1 all-gather.4
